TPU v7x, 32 devices: a whole 2x2x4 slice. The times are simulated.
32 devices in a mesh: space: 16 (over z, y, x), tm: 2 (over core).
Axes of the slice: x: 2, y: 2, z: 4, core: 2. Of those that a mesh axis runs over, the one named last changes fastest.
Arguments:
- right_side: float32 [64, 128, 512], P('tm', 'space'), may hold values from -70 to 70
- kappa_field: float32 [128, 512], P('space'), may hold values from 0.1 to 2
- land_mask: int32 [128, 512], P('space'), may hold values 0 or 1
- nugget: float32 [64], P('tm'), may hold values from 0.5 to 2
- time_band: float32 [5, 64], P(None, 'tm'), may hold values from -0.22 to 1.5, as said below
- taper_width: int32 [8], replicated, may hold values from 1 to 4, as said below
Outputs:
- solution_field: float32 [64, 128, 512], P('tm', 'space')
- residual: float32 [64, 128, 512], P('tm', 'space')
Inputs may be any that keep to these rules, and one draw needn't show every extreme that they name: `time_band`: row 0 holds the diagonal at each hour; row l holds the coupling between hour t and hour t + l, zero where t + l is past the last hour. `taper_width`: some block has width 4 and some block has width 1.
All inputs are finite; a program needn't handle non-finite values. No bound on the sum of `land_mask` on one device may be relied on, other than what follows from the above.
Results may differ from a plain program's by a relative error of at most 0.034.
Values sent between devices are 32-bit elements; how exact they have to be, the bound alone decides.
A program may use at most 64 MiB of HBM per device.

v0:
```python
import jax
import jax.numpy as jnp
from jax import lax
from jax.sharding import PartitionSpec as P

TAPER_HOURS = 8
ITERS = 2


spde_scale = 0.0625


def shifted(shard, axis, by):
    count = lax.axis_size(axis)
    pairs = [(i, i + by) for i in range(count) if 0 <= i + by < count]
    return lax.ppermute(shard, axis, pairs)


def padded_2(block, sides, width):
    for axis, dim in sides:
        count = lax.axis_size(axis)
        forward = [(i, i + 1) for i in range(count - 1)]
        backward = [(target, source) for source, target in forward]
        low = lax.ppermute(
            lax.slice_in_dim(block, block.shape[dim] - width, None, axis=dim), axis, forward
        )
        high = lax.ppermute(lax.slice_in_dim(block, 0, width, axis=dim), axis, backward)
        block = jnp.concatenate([low, block, high], axis=dim)
    return block


def screened_laplace(padded, kappa_rows):
    centre = padded[:, 1:-1, :]
    zero_column = jnp.zeros_like(centre[:, :, :1])
    across = jnp.concatenate([centre[:, :, 1:], zero_column], axis=2) + jnp.concatenate(
        [zero_column, centre[:, :, :-1]], axis=2
    )
    return (kappa_rows + 4.0) * centre - (padded[:, 2:, :] + padded[:, :-2, :] + across)


def tapered_band(time_band, taper_width, first_hour):
    lag_count = time_band.shape[0] - 1
    hour_count = time_band.shape[1]
    lag_values = jnp.arange(1, lag_count + 1, dtype=jnp.int32).astype(jnp.float32)[:, None]
    block_ids = jnp.arange(taper_width.shape[0], dtype=jnp.int32)
    hour_block = (first_hour + jnp.arange(hour_count, dtype=jnp.int32)) // TAPER_HOURS
    hour_width = jnp.sum(
        jnp.where(hour_block[:, None] == block_ids[None, :], taper_width[None, :], 0), axis=1
    )
    taper_factor = jnp.maximum(
        1.0 - lag_values / (hour_width.astype(jnp.float32)[None, :] + 1.0), 0.0
    )
    return time_band[1:] * taper_factor


def temporal_band(padded, diagonal, upper_band, lower_band):
    lag_count = upper_band.shape[0]
    hour_count = upper_band.shape[1]
    summed = diagonal[:, None, None] * padded[lag_count : lag_count + hour_count]
    for lag_step in range(1, lag_count + 1):
        ahead = padded[lag_count + lag_step : lag_count + lag_step + hour_count]
        behind = padded[lag_count - lag_step : lag_count - lag_step + hour_count]
        earlier = lower_band[lag_step - 1, lag_count - lag_step : lag_count - lag_step + hour_count]
        summed = (
            summed
            + upper_band[lag_step - 1][:, None, None] * ahead
            + earlier[:, None, None] * behind
        )
    return summed


def body(right_side, kappa_field, land_mask, nugget, time_band, taper_width):
    hour_count = right_side.shape[0]
    lag_count = time_band.shape[0] - 1
    first_hour = lax.axis_index("tm") * hour_count
    upper_band = tapered_band(time_band, taper_width, first_hour)
    earlier_band = shifted(upper_band[:, hour_count - lag_count :], "tm", 1)
    lower_band = jnp.concatenate([earlier_band, upper_band], axis=1)
    diagonal = time_band[0]
    land_weight = land_mask.astype(jnp.float32)

    def rows_rim(grid_values):
        return padded_2(grid_values, (("space", 1),), 1)

    solution = jnp.zeros_like(right_side)
    residual = right_side
    direction = right_side
    norm_now = lax.psum(jnp.sum(residual * residual), ("space", "tm"))
    for iteration in range(ITERS):
        first_pass = screened_laplace(rows_rim(direction), kappa_field)
        smoothed = spde_scale * screened_laplace(rows_rim(first_pass), kappa_field)
        padded = padded_2(smoothed, (("tm", 0),), lag_count)
        applied = temporal_band(padded, diagonal, upper_band, lower_band) + nugget[
            :, None, None
        ] * (land_weight * direction)
        step_size = norm_now / lax.psum(jnp.sum(direction * applied), ("space", "tm"))
        solution = solution + step_size * direction
        residual = residual - step_size * applied
        if iteration + 1 < ITERS:
            norm_next = lax.psum(jnp.sum(residual * residual), ("space", "tm"))
            direction = residual + norm_next / norm_now * direction
            norm_now = norm_next
    return (solution, residual)


def solution(mesh):
    return jax.shard_map(
        body,
        mesh=mesh,
        in_specs=(
            P("tm", "space", None),
            P("space", None),
            P("space", None),
            P("tm"),
            P(None, "tm"),
            P(),
        ),
        out_specs=(P("tm", "space", None), P("tm", "space", None)),
        check_vma=False,
    )
```

profile of v0, /device:TPU:0, one launch (start us, length us, event | category | flops | bytes accessed | tf_op | source)
XLA Modules:
  0.0 193.4 jit_solution(6829409684401655762)
XLA Ops:
  0.6 0.0 copy-start.5
  0.7 0.0 copy-start.4
  0.7 0.6 copy-done.5
  1.3 0.1 select_reduce_fusion
  1.4 0.0 copy-done.4
  1.4 0.1 fusion.59
  1.5 0.1 slice.214
  1.5 2.3 %collective-permute-start.5 = (f32[4,4]{1,0:T(4,128)S(1)}, f32[4,4]{1,0:T(4,128)S(1)}, u32[]{:S(2)}, u32[]{:S(2)}) collective-permute-start(f32[4,4]{1,0:T(4,128)S(1)} %slice.214), channel_id=1, source_target_pairs={{0,1},{2,3},{4,5},{6,7},{8,9},{10,11},{12,13},{14,15},{16,17},{18,... | collective-permute-start | bytes 200 | tf_op jit(solution)/shard_map/ppermute | solution.py:16
  3.9 1.4 fusion.73
  5.3 1.3 collective-permute-start
  6.6 4.9 %collective-permute-start.1 = (f32[32,1,512]{2,1,0:T(1,128)S(1)}, f32[32,1,512]{2,1,0:T(1,128)S(1)}, u32[]{:S(2)}, u32[]{:S(2)}) collective-permute-start(f32[32,1,512]{2,1,0:T(1,128)S(1)} %get-tuple-element.34), channel_id=1, source_target_pairs={{0,2},{2,4},{4,6},{6,8},{8,10},{10,12},{12,14},{14,16},{16,18},{18... | collective-permute-start | bytes 196616 | tf_op jit(solution)/shard_map/ppermute | solution.py:24
  11.5 0.0 copy-start.1
  11.5 0.0 copy-start
  11.5 1.5 fusion.72
  13.0 0.0 copy-done.1
  13.0 0.0 copy-start.2
  13.0 0.7 copy-done.2
  13.7 0.0 collective-permute-done.5
  13.7 0.1 pad_maximum_fusion.12
  13.8 0.0 collective-permute-done
  13.8 0.0 collective-permute-done.1
  13.8 0.0 copy-done
  13.8 0.3 fusion.57
  14.2 0.1 fusion.70
  14.3 1.3 collective-permute-start.2
  15.6 5.4 %collective-permute-start.3 = (f32[32,1,512]{2,1,0:T(1,128)S(1)}, f32[32,1,512]{2,1,0:T(1,128)S(1)}, u32[]{:S(2)}, u32[]{:S(2)}) collective-permute-start(f32[32,1,512]{2,1,0:T(1,128)S(1)} %get-tuple-element.28), channel_id=1, source_target_pairs={{0,2},{2,4},{4,6},{6,8},{8,10},{10,12},{12,14},{14,16},{16,18},{18... | collective-permute-start | bytes 196616 | tf_op jit(solution)/shard_map/ppermute | solution.py:24
  21.0 0.2 fusion.71
  21.2 0.1 collective-permute-done.2
  21.3 1.6 collective-permute-done.3
  22.9 0.3 broadcast_multiply_fusion.1
  23.3 1.3 collective-permute-start.4
  24.6 3.0 %collective-permute-start.6 = (f32[4,8,512]{2,1,0:T(8,128)S(1)}, f32[4,8,512]{2,1,0:T(8,128)S(1)}, u32[]{:S(2)}, u32[]{:S(2)}) collective-permute-start(f32[4,8,512]{2,1,0:T(8,128)S(1)} %get-tuple-element.26), channel_id=1, source_target_pairs={{0,1},{2,3},{4,5},{6,7},{8,9},{10,11},{12,13},{14,15},{16,17},{18,... | collective-permute-start | bytes 196616 | tf_op jit(solution)/shard_map/ppermute | solution.py:24
  27.6 0.1 slice_bitcast_fusion.6
  27.7 0.0 collective-permute-done.4
  27.7 0.8 collective-permute-done.6
  28.5 0.0 copy-start.3
  28.5 0.7 copy-done.3
  29.1 1.7 multiply_reduce_fusion.2
  30.8 45.7 %all-reduce.8 = (f32[]{:T(128)}, f32[]{:T(128)}) all-reduce(f32[]{:T(128)} %get-tuple-element.3, f32[]{:T(128)} %get-tuple-element.2), channel_id=1, replica_groups=mesh['space'=16,'tm'=2] {'space','tm'}, use_global_device_ids=true, to_apply=%region_1.2 | all-reduce | flops 2 | bytes 16 | tf_op jit(solution)/shard_map/psum | solution.py:88
  77.9 0.8 multiply_reduce_fusion.1
  78.6 40.2 %psum.30 = f32[]{:T(128)} all-reduce(f32[]{:T(128)} %multiply_reduce_fusion.1), channel_id=1, replica_groups=mesh['space'=16,'tm'=2] {'space','tm'}, use_global_device_ids=true, to_apply=%region_6.7 | all-reduce | flops 1 | bytes 8 | tf_op jit(solution)/shard_map/psum | solution.py:100
  120.2 0.1 multiply_add_fusion.1
  120.3 0.1 fusion.68
  120.4 1.3 collective-permute-start.7
  121.7 4.8 %collective-permute-start.8 = (f32[32,1,512]{2,1,0:T(1,128)S(1)}, f32[32,1,512]{2,1,0:T(1,128)S(1)}, u32[]{:S(2)}, u32[]{:S(2)}) collective-permute-start(f32[32,1,512]{2,1,0:T(1,128)S(1)} %get-tuple-element.24), channel_id=1, source_target_pairs={{0,2},{2,4},{4,6},{6,8},{8,10},{10,12},{12,14},{14,16},{16,18},{18... | collective-permute-start | bytes 196616 | tf_op jit(solution)/shard_map/ppermute | solution.py:24
  126.5 0.2 fusion.67
  126.7 0.1 collective-permute-done.7
  126.8 2.2 %collective-permute-done.8 = f32[32,1,512]{2,1,0:T(1,128)S(1)} collective-permute-done((f32[32,1,512]{2,1,0:T(1,128)S(1)}, f32[32,1,512]{2,1,0:T(1,128)S(1)}, u32[]{:S(2)}, u32[]{:S(2)}) %collective-permute-start.8) | collective-permute-done | bytes 65568 | tf_op jit(solution)/shard_map/ppermute | solution.py:24
  129.0 0.3 fusion.49
  129.4 0.1 fusion.65
  129.4 1.3 collective-permute-start.9
  130.7 5.0 %collective-permute-start.10 = (f32[32,1,512]{2,1,0:T(1,128)S(1)}, f32[32,1,512]{2,1,0:T(1,128)S(1)}, u32[]{:S(2)}, u32[]{:S(2)}) collective-permute-start(f32[32,1,512]{2,1,0:T(1,128)S(1)} %get-tuple-element.18), channel_id=1, source_target_pairs={{0,2},{2,4},{4,6},{6,8},{8,10},{10,12},{12,14},{14,16},{16,18},{18... | collective-permute-start | bytes 196616 | tf_op jit(solution)/shard_map/ppermute | solution.py:24
  135.7 0.2 fusion.66
  135.9 0.1 collective-permute-done.9
  136.0 1.6 collective-permute-done.10
  137.6 0.3 broadcast_multiply_fusion
  138.0 1.3 collective-permute-start.11
  139.3 3.0 %collective-permute-start.12 = (f32[4,8,512]{2,1,0:T(8,128)S(1)}, f32[4,8,512]{2,1,0:T(8,128)S(1)}, u32[]{:S(2)}, u32[]{:S(2)}) collective-permute-start(f32[4,8,512]{2,1,0:T(8,128)S(1)} %get-tuple-element.16), channel_id=1, source_target_pairs={{0,1},{2,3},{4,5},{6,7},{8,9},{10,11},{12,13},{14,15},{16,17},{18,... | collective-permute-start | bytes 196616 | tf_op jit(solution)/shard_map/ppermute | solution.py:24
  142.3 0.0 collective-permute-done.11
  142.3 0.9 collective-permute-done.12
  143.2 1.7 multiply_reduce_fusion
  144.9 45.9 %psum.31 = f32[]{:T(128)} all-reduce(f32[]{:T(128)} %get-tuple-element.6), channel_id=1, replica_groups=mesh['space'=16,'tm'=2] {'space','tm'}, use_global_device_ids=true, to_apply=%region_8.9 | all-reduce | flops 1 | bytes 8 | tf_op jit(solution)/shard_map/psum | solution.py:96
  192.1 1.2 multiply_subtract_fusion
  (9 shorter events, 0.1 us)
Async XLA Ops:
  0.6 0.7 copy-start.5
  0.7 0.7 copy-start.4
  1.5 12.2 %collective-permute-start.5 = (f32[4,4]{1,0:T(4,128)S(1)}, f32[4,4]{1,0:T(4,128)S(1)}, u32[]{:S(2)}, u32[]{:S(2)}) collective-permute-start(f32[4,4]{1,0:T(4,128)S(1)} %slice.214), channel_id=1, source_target_pairs={{0,1},{2,3},{4,5},{6,7},{8,9},{10,11},{12,13},{14,15},{16,17},{18,... | collective-permute-start | bytes 200 | tf_op jit(solution)/shard_map/ppermute | solution.py:16
  5.3 8.5 %collective-permute-start = (f32[32,1,512]{2,1,0:T(1,128)S(1)}, f32[32,1,512]{2,1,0:T(1,128)S(1)}, u32[]{:S(2)}, u32[]{:S(2)}) collective-permute-start(f32[32,1,512]{2,1,0:T(1,128)S(1)} %get-tuple-element.33), channel_id=1, source_target_pairs={{2,0},{4,2},{6,4},{8,6},{10,8},{12,10},{14,12},{16,14},{18,16},{20... | collective-permute-start | bytes 196616 | tf_op jit(solution)/shard_map/ppermute | solution.py:27
  6.6 7.3 %collective-permute-start.1 = (f32[32,1,512]{2,1,0:T(1,128)S(1)}, f32[32,1,512]{2,1,0:T(1,128)S(1)}, u32[]{:S(2)}, u32[]{:S(2)}) collective-permute-start(f32[32,1,512]{2,1,0:T(1,128)S(1)} %get-tuple-element.34), channel_id=1, source_target_pairs={{0,2},{2,4},{4,6},{6,8},{8,10},{10,12},{12,14},{14,16},{16,18},{18... | collective-permute-start | bytes 196616 | tf_op jit(solution)/shard_map/ppermute | solution.py:24
  11.5 1.5 copy-start.1
  11.5 2.4 %copy-start = (f32[32,8,512]{2,1,0:T(8,128)S(1)}, f32[32,8,512]{2,1,0:T(8,128)}, u32[]{:S(2)}) copy-start(f32[32,8,512]{2,1,0:T(8,128)} %param.6) | copy-start | bytes 1572868
  13.0 0.7 copy-start.2
  14.3 7.0 %collective-permute-start.2 = (f32[32,1,512]{2,1,0:T(1,128)S(1)}, f32[32,1,512]{2,1,0:T(1,128)S(1)}, u32[]{:S(2)}, u32[]{:S(2)}) collective-permute-start(f32[32,1,512]{2,1,0:T(1,128)S(1)} %get-tuple-element.27), channel_id=1, source_target_pairs={{2,0},{4,2},{6,4},{8,6},{10,8},{12,10},{14,12},{16,14},{18,16},{20... | collective-permute-start | bytes 196616 | tf_op jit(solution)/shard_map/ppermute | solution.py:27
  15.6 7.3 %collective-permute-start.3 = (f32[32,1,512]{2,1,0:T(1,128)S(1)}, f32[32,1,512]{2,1,0:T(1,128)S(1)}, u32[]{:S(2)}, u32[]{:S(2)}) collective-permute-start(f32[32,1,512]{2,1,0:T(1,128)S(1)} %get-tuple-element.28), channel_id=1, source_target_pairs={{0,2},{2,4},{4,6},{6,8},{8,10},{10,12},{12,14},{14,16},{16,18},{18... | collective-permute-start | bytes 196616 | tf_op jit(solution)/shard_map/ppermute | solution.py:24
  23.3 4.4 %collective-permute-start.4 = (f32[4,8,512]{2,1,0:T(8,128)S(1)}, f32[4,8,512]{2,1,0:T(8,128)S(1)}, u32[]{:S(2)}, u32[]{:S(2)}) collective-permute-start(f32[4,8,512]{2,1,0:T(8,128)S(1)} %get-tuple-element.25), channel_id=1, source_target_pairs={{1,0},{3,2},{5,4},{7,6},{9,8},{11,10},{13,12},{15,14},{17,16},{19,... | collective-permute-start | bytes 196616 | tf_op jit(solution)/shard_map/ppermute | solution.py:27
  24.6 3.9 %collective-permute-start.6 = (f32[4,8,512]{2,1,0:T(8,128)S(1)}, f32[4,8,512]{2,1,0:T(8,128)S(1)}, u32[]{:S(2)}, u32[]{:S(2)}) collective-permute-start(f32[4,8,512]{2,1,0:T(8,128)S(1)} %get-tuple-element.26), channel_id=1, source_target_pairs={{0,1},{2,3},{4,5},{6,7},{8,9},{10,11},{12,13},{14,15},{16,17},{18,... | collective-permute-start | bytes 196616 | tf_op jit(solution)/shard_map/ppermute | solution.py:24
  28.5 0.7 copy-start.3
  120.4 6.4 %collective-permute-start.7 = (f32[32,1,512]{2,1,0:T(1,128)S(1)}, f32[32,1,512]{2,1,0:T(1,128)S(1)}, u32[]{:S(2)}, u32[]{:S(2)}) collective-permute-start(f32[32,1,512]{2,1,0:T(1,128)S(1)} %get-tuple-element.23), channel_id=1, source_target_pairs={{2,0},{4,2},{6,4},{8,6},{10,8},{12,10},{14,12},{16,14},{18,16},{20... | collective-permute-start | bytes 196616 | tf_op jit(solution)/shard_map/ppermute | solution.py:27
  121.7 7.3 %collective-permute-start.8 = (f32[32,1,512]{2,1,0:T(1,128)S(1)}, f32[32,1,512]{2,1,0:T(1,128)S(1)}, u32[]{:S(2)}, u32[]{:S(2)}) collective-permute-start(f32[32,1,512]{2,1,0:T(1,128)S(1)} %get-tuple-element.24), channel_id=1, source_target_pairs={{0,2},{2,4},{4,6},{6,8},{8,10},{10,12},{12,14},{14,16},{16,18},{18... | collective-permute-start | bytes 196616 | tf_op jit(solution)/shard_map/ppermute | solution.py:24
  129.4 6.6 %collective-permute-start.9 = (f32[32,1,512]{2,1,0:T(1,128)S(1)}, f32[32,1,512]{2,1,0:T(1,128)S(1)}, u32[]{:S(2)}, u32[]{:S(2)}) collective-permute-start(f32[32,1,512]{2,1,0:T(1,128)S(1)} %get-tuple-element.17), channel_id=1, source_target_pairs={{2,0},{4,2},{6,4},{8,6},{10,8},{12,10},{14,12},{16,14},{18,16},{20... | collective-permute-start | bytes 196616 | tf_op jit(solution)/shard_map/ppermute | solution.py:27
  130.7 6.9 %collective-permute-start.10 = (f32[32,1,512]{2,1,0:T(1,128)S(1)}, f32[32,1,512]{2,1,0:T(1,128)S(1)}, u32[]{:S(2)}, u32[]{:S(2)}) collective-permute-start(f32[32,1,512]{2,1,0:T(1,128)S(1)} %get-tuple-element.18), channel_id=1, source_target_pairs={{0,2},{2,4},{4,6},{6,8},{8,10},{10,12},{12,14},{14,16},{16,18},{18... | collective-permute-start | bytes 196616 | tf_op jit(solution)/shard_map/ppermute | solution.py:24
  138.0 4.3 %collective-permute-start.11 = (f32[4,8,512]{2,1,0:T(8,128)S(1)}, f32[4,8,512]{2,1,0:T(8,128)S(1)}, u32[]{:S(2)}, u32[]{:S(2)}) collective-permute-start(f32[4,8,512]{2,1,0:T(8,128)S(1)} %get-tuple-element.15), channel_id=1, source_target_pairs={{1,0},{3,2},{5,4},{7,6},{9,8},{11,10},{13,12},{15,14},{17,16},{19,... | collective-permute-start | bytes 196616 | tf_op jit(solution)/shard_map/ppermute | solution.py:27
  139.3 3.9 %collective-permute-start.12 = (f32[4,8,512]{2,1,0:T(8,128)S(1)}, f32[4,8,512]{2,1,0:T(8,128)S(1)}, u32[]{:S(2)}, u32[]{:S(2)}) collective-permute-start(f32[4,8,512]{2,1,0:T(8,128)S(1)} %get-tuple-element.16), channel_id=1, source_target_pairs={{0,1},{2,3},{4,5},{6,7},{8,9},{10,11},{12,13},{14,15},{16,17},{18,... | collective-permute-start | bytes 196616 | tf_op jit(solution)/shard_map/ppermute | solution.py:24
where the time goes:
time: 194 us; the launch traced here: 193 us
  blocking collectives  132 us (68%)
  starting transfers between devices  36.3 us (19%)
  waiting for transfers between devices  7.35 us (4%)
  other arithmetic  7.1 us (4%)
  local copies, waits for them, and re-layouts  5.92 us (3%)
  between operations  4.93 us (3%)
    psum x1, blocking collectives, body(): lax.psum(jnp.sum(direction * applied), ('space', 'tm'))  45.9 us
    psum x1, blocking collectives, body(): norm_now = lax.psum(jnp.sum(residual * residual), ('space', 'tm'))  45.7 us
    psum x1, blocking collectives, body(): norm_next = lax.psum(jnp.sum(residual * residual), ('space', 'tm'))  40.2 us
    ppermute x6, starting transfers between devices, padded_2(): lax.ppermute(lax.slice_in_dim(block, block.shape[dim] - width, None, axis...  26.1 us
    ppermute x6, starting transfers between devices, padded_2(): lax.ppermute(lax.slice_in_dim(block, 0, width, axis=dim), axis, backward)  7.75 us
    ppermute x6, waiting for transfers between devices, padded_2(): lax.ppermute(lax.slice_in_dim(block, block.shape[dim] - width, None, axis...  7.06 us
  transfers between devices with their start and end apart: 13, of which 8 were waited for; matrix products, arithmetic and copies ran while one was open for 2% of the time, Pallas kernels for 0%

commit v1 on v0

v1 whole, which is shorter than its diff:
```python
import functools

import jax
import jax.numpy as jnp
from jax import lax
from jax.experimental import pallas as pl
from jax.experimental.pallas import tpu as pltpu
from jax.sharding import PartitionSpec as P

TAPER_HOURS = 8
LAG = 4
RIM = 2
LOW = 4

SPDE_SCALE = 0.0625
MESH = pl.DeviceIdType.MESH


def halo_offsets():
    return [(1, 0), (-1, 0), (1, 1), (1, -1), (-1, 1), (-1, -1), (0, 1), (0, -1)]


def kernel(
    ns,
    nt,
    right_ref,
    kappa_ref,
    mask_ref,
    nugget_ref,
    band_ref,
    taper_ref,
    q_out,
    w_ref,
    coef_ref,
    b_pad,
    b_rim,
    q_pad,
    q_rim,
    mixed,
    band,
    kappa_rim,
    sum_near,
    sum_far,
    local_sem,
    halo_send,
    halo_recv,
    aux_send,
    aux_recv,
    near_send,
    near_recv,
    far_send,
    far_recv,
):
    s = lax.axis_index("space")
    t = lax.axis_index("tm")
    hours = w_ref.shape[0]
    rows = w_ref.shape[1]
    cols = w_ref.shape[2]
    low = min(LOW, ns)
    near = low * nt
    far = ns // low

    load_b = pltpu.make_async_copy(right_ref, b_pad.at[pl.ds(LAG, hours)], local_sem.at[0])
    load_b.start()

    def near_partner(k):
        me = (s % low) * nt + t
        other = (me + k) % near
        return (s // low) * low + other // nt, other % nt

    def far_partner(k):
        other = (s // low + k) % far
        return other * low + s % low, t

    def exists(ds, dt):
        ok = None
        for pos, step, count in ((s, ds, ns), (t, dt, nt)):
            if step:
                here = pos < count - 1 if step > 0 else pos > 0
                ok = here if ok is None else jnp.logical_and(ok, here)
        return ok

    b_rim[...] = jnp.zeros_like(b_rim)
    q_rim[...] = jnp.zeros_like(q_rim)
    kappa_rim[...] = jnp.zeros_like(kappa_rim)
    edge = jnp.zeros((LAG, rows, cols), jnp.float32)
    for pad in (b_pad, q_pad):
        pad[0:LAG] = edge
        pad[LAG + hours : LAG + hours + LAG] = edge
    band[0:LAG] = jnp.zeros((LAG, 8, 128), jnp.float32)

    barrier = pltpu.get_barrier_semaphore()
    greeted = jnp.int32(near - 1 + far - 1)
    for ds, dt in halo_offsets():
        here = exists(ds, dt)
        greeted = greeted + here.astype(jnp.int32)

        @pl.when(here)
        def _():
            pl.semaphore_signal(barrier, inc=1, device_id=(s + ds, t + dt), device_id_type=MESH)

    for k in range(1, near):
        pl.semaphore_signal(barrier, inc=1, device_id=near_partner(k), device_id_type=MESH)
    for k in range(1, far):
        pl.semaphore_signal(barrier, inc=1, device_id=far_partner(k), device_id_type=MESH)

    lag_row = lax.broadcasted_iota(jnp.int32, (8, 128), 0)
    lag_value = lag_row.astype(jnp.float32)

    def fill_band(h, carry):
        width = taper_ref[(t * hours + h) // TAPER_HOURS].astype(jnp.float32)
        taper = jnp.maximum(1.0 - lag_value / (jnp.full((8, 128), width) + 1.0), 0.0)
        value = jnp.zeros((8, 128), jnp.float32)
        for l in range(LAG + 1):
            value = jnp.where(lag_row == l, band_ref[l, h], value)
        value = value * taper
        band[LAG + h] = jnp.where(lag_row == LAG + 1, nugget_ref[h], value)
        return carry

    lax.fori_loop(0, hours, fill_band, 0)

    load_b.wait()
    pl.semaphore_wait(barrier, greeted)

    row_of = {1: pl.ds(rows - RIM, RIM), -1: pl.ds(0, RIM)}
    hour_from = {0: pl.ds(LAG, hours), 1: pl.ds(hours, LAG), -1: pl.ds(LAG, LAG)}
    hour_to = {0: pl.ds(LAG, hours), 1: pl.ds(0, LAG), -1: pl.ds(LAG + hours, LAG)}

    def halo_copy(which, index, pad, rim):
        ds, dt = halo_offsets()[index]
        if ds:
            source = pad.at[hour_from[dt], row_of[ds]]
            target = rim.at[hour_to[dt], row_of[ds]]
        else:
            source = pad.at[hour_from[dt]]
            target = pad.at[hour_to[dt]]
        return pltpu.make_async_remote_copy(
            src_ref=source,
            dst_ref=target,
            send_sem=halo_send.at[which, index],
            recv_sem=halo_recv.at[which, index],
            device_id=(s + ds, t + dt),
            device_id_type=MESH,
        )

    def aux_copies():
        out = []
        for n, (ds, row) in enumerate(((1, rows - 1), (-1, 0))):
            out.append((
                ds,
                0,
                pltpu.make_async_remote_copy(
                    src_ref=kappa_ref.at[pl.ds(row, 1)],
                    dst_ref=kappa_rim.at[pl.ds(row, 1)],
                    send_sem=aux_send.at[n],
                    recv_sem=aux_recv.at[n],
                    device_id=(s + ds, t),
                    device_id_type=MESH,
                ),
            ))
        out.append((
            0,
            1,
            pltpu.make_async_remote_copy(
                src_ref=band.at[pl.ds(hours, LAG)],
                dst_ref=band.at[pl.ds(0, LAG)],
                send_sem=aux_send.at[2],
                recv_sem=aux_recv.at[2],
                device_id=(s, t + 1),
                device_id_type=MESH,
            ),
        ))
        return out

    def start_halo(which, pad, rim):
        for index, (ds, dt) in enumerate(halo_offsets()):

            @pl.when(exists(ds, dt))
            def _():
                halo_copy(which, index, pad, rim).start()

    def wait_halo(which, pad, rim, along_hours):
        for index, (ds, dt) in enumerate(halo_offsets()):
            if (ds == 0) == along_hours:

                @pl.when(exists(-ds, -dt))
                def _():
                    halo_copy(which, index, pad, rim).wait_recv()

    def drain_halo(which, pad, rim):
        for index, (ds, dt) in enumerate(halo_offsets()):

            @pl.when(exists(ds, dt))
            def _():
                halo_copy(which, index, pad, rim).wait_send()

    start_halo(0, b_pad, b_rim)
    for ds, dt, copy in aux_copies():

        @pl.when(exists(ds, dt))
        def _():
            copy.start()

    grid_row = lax.broadcasted_iota(jnp.int32, (rows, cols), 0)
    grid_col = lax.broadcasted_iota(jnp.int32, (rows, cols), 1)
    first_row = grid_row == 0
    last_row = grid_row == rows - 1
    first_col = grid_col == 0
    last_col = grid_col == cols - 1

    def coupling(h, row):
        return jnp.concatenate([band[h, pl.ds(row, 1), :]] * (cols // 128), axis=1)

    def along_time(field, h):
        total = coupling(LAG + h, 0) * field[LAG + h]
        for l in range(1, LAG + 1):
            total = (
                total
                + coupling(LAG + h, l) * field[LAG + h + l]
                + coupling(LAG + h - l, l) * field[LAG + h - l]
            )
        return total

    def laplace(x, rim, kappa4):
        above = pltpu.roll(jnp.where(last_row, rim, x), 1, 0)
        below = pltpu.roll(jnp.where(first_row, rim, x), rows - 1, 0)
        left = jnp.where(first_col, 0.0, pltpu.roll(x, 1, 1))
        right = jnp.where(last_col, 0.0, pltpu.roll(x, cols - 1, 1))
        return kappa4 * x - ((above + below) + (left + right))

    def mix_hours(pad):
        def step(h, carry):
            mixed[h] = along_time(pad, h)
            return carry

        lax.fori_loop(0, hours, step, 0, unroll=2)

    def image(pad, rim, h):
        x = mixed[h]
        x_rim = along_time(rim, h)
        kappa4 = kappa_ref[...] + 4.0
        kappa4_rim = kappa_rim[...] + 4.0
        inside = jnp.logical_or(
            jnp.logical_and(last_row, s > 0), jnp.logical_and(first_row, s < ns - 1)
        )
        y = laplace(x, x_rim, kappa4)
        y_rim = jnp.where(inside, laplace(x_rim, x, kappa4_rim), 0.0)
        z = laplace(y, y_rim, kappa4)
        weight = coupling(LAG + h, LAG + 1) * mask_ref[...].astype(jnp.float32)
        return SPDE_SCALE * z + weight * pad[LAG + h]

    def fold(x):
        out = x[:, :128]
        for c in range(128, cols, 128):
            out = out + x[:, c : c + 128]
        return out

    def start_sum(which, buffers, sends, recvs, me, size, partner):
        copies = []
        for k in range(1, size):
            copy = pltpu.make_async_remote_copy(
                src_ref=buffers.at[which, me],
                dst_ref=buffers.at[which, me],
                send_sem=sends.at[which, k],
                recv_sem=recvs.at[which, k],
                device_id=partner(k),
                device_id_type=MESH,
            )
            copy.start()
            copies.append(copy)
        return copies

    near_me = (s % low) * nt + t
    far_me = s // low

    def start_near(which, first, second):
        one = jnp.sum(first, axis=0, keepdims=True)
        two = jnp.sum(second, axis=0, keepdims=True)
        value = jnp.where(lag_row == 0, one, jnp.where(lag_row == 1, two, 0.0))
        sum_near[which, near_me] = value
        return start_sum(which, sum_near, near_send, near_recv, near_me, near, near_partner)

    def finish_near(which, copies):
        for copy in copies:
            copy.wait()
        total = sum_near[which, 0]
        for k in range(1, near):
            total = total + sum_near[which, k]
        return total

    def start_far(which, value):
        sum_far[which, far_me] = value
        return start_sum(which, sum_far, far_send, far_recv, far_me, far, far_partner)

    def finish_far(which, copies):
        for copy in copies:
            copy.wait()
        total = sum_far[which, 0]
        for k in range(1, far):
            total = total + sum_far[which, k]
        total = jnp.sum(total, axis=1, keepdims=True)
        return total[0:1, :], total[1:2, :]

    wait_halo(0, b_pad, b_rim, True)
    for ds, dt, copy in aux_copies():

        @pl.when(exists(-ds, -dt))
        def _():
            copy.wait_recv()

    mix_hours(b_pad)
    wait_halo(0, b_pad, b_rim, False)

    def first_step(h, carry):
        norm, product = carry
        value = image(b_pad, b_rim, h)
        q_pad[LAG + h] = value
        b = b_pad[LAG + h]
        return norm + fold(b * b), product + fold(b * value)

    zero = jnp.zeros((rows, 128), jnp.float32)
    norm, product = lax.fori_loop(0, hours, first_step, (zero, zero), unroll=2)

    start_halo(1, q_pad, q_rim)
    copies = start_near(0, norm, product)
    store_q = pltpu.make_async_copy(q_pad.at[pl.ds(LAG, hours)], q_out, local_sem.at[1])
    store_q.start()
    drain_halo(0, b_pad, b_rim)
    for ds, dt, copy in aux_copies():

        @pl.when(exists(ds, dt))
        def _():
            copy.wait_send()

    wait_halo(1, q_pad, q_rim, True)
    value = finish_near(0, copies)
    copies = start_far(0, value)
    mix_hours(q_pad)
    norm_0, product_0 = finish_far(0, copies)
    step_0 = norm_0 / product_0
    wait_halo(1, q_pad, q_rim, False)

    def second_step(h, carry):
        norm, product = carry
        q = q_pad[LAG + h]
        value = image(q_pad, q_rim, h)
        w_ref[h] = value
        left = b_pad[LAG + h] - step_0 * q
        left_image = q - step_0 * value
        return norm + fold(left * left), product + fold(left * left_image)

    norm, product = lax.fori_loop(0, hours, second_step, (zero, zero), unroll=2)
    copies = start_near(1, norm, product)
    drain_halo(1, q_pad, q_rim)
    store_q.wait()
    value = finish_near(1, copies)
    copies = start_far(1, value)
    norm_1, product_1 = finish_far(1, copies)

    ratio = norm_1 / norm_0
    step_1 = norm_1 / (product_1 - ratio * norm_1 / step_0)
    scale_1 = step_0 + step_1 * (1.0 + ratio)
    scale_2 = step_1 * step_0
    coef_ref[...] = jnp.where(lag_row == 0, scale_1, scale_2)


def body(ns, nt, right_side, kappa_field, land_mask, nugget, time_band, taper_width):
    hours, rows, cols = right_side.shape
    low = min(LOW, ns)
    near = low * nt
    far = ns // low
    padded = pltpu.VMEM((hours + 2 * LAG, rows, cols), jnp.float32)
    vmem = pl.BlockSpec(memory_space=pltpu.VMEM)
    smem = pl.BlockSpec(memory_space=pltpu.SMEM)
    hbm = pl.BlockSpec(memory_space=pl.ANY)
    field = jax.ShapeDtypeStruct(right_side.shape, jnp.float32)
    q, w, coef = pl.pallas_call(
        functools.partial(kernel, ns, nt),
        out_shape=(field, field, jax.ShapeDtypeStruct((8, 128), jnp.float32)),
        in_specs=[hbm, vmem, vmem, smem, smem, smem],
        out_specs=(hbm, vmem, vmem),
        scratch_shapes=[
            padded,
            padded,
            padded,
            padded,
            pltpu.VMEM((hours, rows, cols), jnp.float32),
            pltpu.VMEM((hours + LAG, 8, 128), jnp.float32),
            pltpu.VMEM((rows, cols), jnp.float32),
            pltpu.VMEM((2, near, 8, 128), jnp.float32),
            pltpu.VMEM((2, far, 8, 128), jnp.float32),
            pltpu.SemaphoreType.DMA((2,)),
            pltpu.SemaphoreType.DMA((2, 8)),
            pltpu.SemaphoreType.DMA((2, 8)),
            pltpu.SemaphoreType.DMA((3,)),
            pltpu.SemaphoreType.DMA((3,)),
            pltpu.SemaphoreType.DMA((2, near)),
            pltpu.SemaphoreType.DMA((2, near)),
            pltpu.SemaphoreType.DMA((2, far)),
            pltpu.SemaphoreType.DMA((2, far)),
        ],
        compiler_params=pltpu.CompilerParams(
            collective_id=0, has_side_effects=True, vmem_limit_bytes=32 * 1024 * 1024
        ),
        cost_estimate=pl.CostEstimate(
            flops=200 * right_side.size, bytes_accessed=12 * right_side.size, transcendentals=0
        ),
    )(right_side, kappa_field, land_mask, nugget, time_band, taper_width)
    scale_1 = coef[0, 0]
    scale_2 = coef[1, 0]
    return (
        scale_1 * right_side - scale_2 * q,
        right_side - scale_1 * q + scale_2 * w,
    )


def solution(mesh):
    return jax.shard_map(
        functools.partial(body, mesh.shape["space"], mesh.shape["tm"]),
        mesh=mesh,
        in_specs=(
            P("tm", "space", None),
            P("space", None),
            P("space", None),
            P("tm"),
            P(None, "tm"),
            P(),
        ),
        out_specs=(P("tm", "space", None), P("tm", "space", None)),
        check_vma=False,
    )
```

time: 194 us -> 48.5 us (0.25)
  blocking collectives: 132 us -> 0 us
  Pallas kernels: 0 us -> 40 us
  starting transfers between devices: 36.3 us -> 0 us
  waiting for transfers between devices: 7.35 us -> 0 us
  other arithmetic: 7.1 us -> 2.46 us
  between operations: 4.93 us -> 0.65 us
    psum x3 -> x0, blocking collectives: 132 us -> none  [the longest x1 45.9 us: body(): lax.psum(jnp.sum(direction * applied), ('space', 'tm'))]
    pallas_call x0 -> x1, Pallas kernels: none -> 40 us  [body(): pl.pallas_call(functools.partial(kernel, ns, nt), out_shape=(field, field...]
    ppermute x13 -> x0, starting transfers between devices: 36.3 us -> none  [the longest x6 26.1 us: padded_2(): lax.ppermute(lax.slice_in_dim(block, block.shape[dim] - width, None, axis...]
    ppermute x13 -> x0, waiting for transfers between devices: 7.35 us -> none  [the longest x6 7.06 us: padded_2(): lax.ppermute(lax.slice_in_dim(block, block.shape[dim] - width, None, axis...]
    reduce_sum x4 -> x0, other arithmetic: 4.27 us -> none  [the longest x2 3.42 us: body(): jnp.sum(direction * applied)]
    slice x11 -> x1, local copies, waits for them, and re-layouts: 3.85 us -> 0.58 us  [body(): scale_1 = coef[0, 0]]
    unnamed x12, local copies, waits for them, and re-layouts: 2 us -> 4.46 us
    add x3 -> x1, other arithmetic: 0.12 us -> 2.46 us  [body(): right_side - scale_1 * q + scale_2 * w]
  transfers between devices with their start and end apart: 13 -> 0, of which waited for: 8 -> 0; matrix products, arithmetic and copies ran while one was open for 2% -> 0% of each run, Pallas kernels for 0% -> 0%
where the time goes in v1:
time: 48.5 us; the launch traced here: 48.1 us
  Pallas kernels  40 us (82%)
  local copies, waits for them, and re-layouts  5.05 us (10%)
  other arithmetic  2.46 us (5%)
  between operations  0.65 us (1%)
    pallas_call x1, Pallas kernels, body(): pl.pallas_call(functools.partial(kernel, ns, nt), out_shape=(field, field...  40 us
    unnamed x12, local copies, waits for them, and re-layouts  4.46 us
    add x1, other arithmetic, body(): right_side - scale_1 * q + scale_2 * w  2.46 us

profile of v1, /device:TPU:0, one launch (start us, length us, event | category | flops | bytes accessed | tf_op | source)
XLA Modules:
  0.0 48.1 jit_solution(2658267432272643892)
XLA Ops:
  0.6 0.0 copy-start
  0.6 1.0 %copy-done = f32[32,8,512]{2,1,0:T(8,128)S(1)} copy-done((f32[32,8,512]{2,1,0:T(8,128)S(1)}, f32[32,8,512]{2,1,0:T(8,128)}, u32[]{:S(2)}) %copy-start) | copy-done | bytes 524312
  1.7 0.0 copy-start.1
  1.7 0.7 %copy-done.1 = f32[8,512]{1,0:T(8,128)S(1)} copy-done((f32[8,512]{1,0:T(8,128)S(1)}, f32[8,512]{1,0:T(8,128)}, u32[]{:S(2)}) %copy-start.1) | copy-done | bytes 16408
  2.4 0.0 copy-start.2
  2.4 0.7 %copy-done.2 = s32[8,512]{1,0:T(8,128)S(1)} copy-done((s32[8,512]{1,0:T(8,128)S(1)}, s32[8,512]{1,0:T(8,128)}, u32[]{:S(2)}) %copy-start.2) | copy-done | bytes 16408
  3.1 0.0 copy-start.3
  3.1 0.7 %copy-done.3 = f32[5,32]{1,0:T(8,128)S(1)} copy-done((f32[5,32]{1,0:T(8,128)S(1)}, f32[5,32]{1,0:T(8,128)}, u32[]{:S(2)}) %copy-start.3) | copy-done | bytes 664
  3.8 0.0 copy-start.4
  3.8 0.7 %copy-done.4 = f32[32]{0:T(128)S(1)} copy-done((f32[32]{0:T(128)S(1)}, f32[32]{0:T(128)}, u32[]{:S(2)}) %copy-start.4) | copy-done | bytes 152
  4.5 0.0 copy-start.5
  4.5 0.7 %copy-done.5 = s32[8]{0:T(128)S(1)} copy-done((s32[8]{0:T(128)S(1)}, s32[8]{0:T(128)}, u32[]{:S(2)}) %copy-start.5) | copy-done | bytes 56
  5.1 40.0 %shard_map.77 = (f32[32,8,512]{2,1,0:T(8,128)S(1)}, f32[32,8,512]{2,1,0:T(8,128)S(1)}, f32[8,128]{1,0:T(8,128)S(1)}) custom-call(f32[32,8,512]{2,1,0:T(8,128)S(1)} %copy-done, f32[8,512]{1,0:T(8,128)S(1)} %copy-done.1, s32[8,512]{1,0:T(8,128)S(1)} %copy-done.2, f32[32]{0:T(128)S(1)} %copy-done.4, f32[5,32]{1,0:T(8,128)S(1)} %copy-done.3, s32[8]{0:T(128)S(1)} %copy-done.5), custom_call_target="tpu_custom_call" | custom-call | flops 26214400 | bytes 1572864 | tf_op jit(solution)/shard_map/pallas_call | solution.py:377
  45.1 0.6 %fusion = (f32[1,1]{1,0:T(1,128)}, f32[1,1]{1,0:T(1,128)}) fusion(f32[8,128]{1,0:T(8,128)S(1)} %get-tuple-element.5), kind=kLoop, calls=%fused_computation.2 | loop fusion | bytes 16 | tf_op jit(solution)/shard_map/slice | solution.py:409
  45.7 2.5 %multiply_add_fusion = (f32[32,8,512]{2,1,0:T(8,128)}, f32[32,8,512]{2,1,0:T(8,128)}) fusion(f32[32,8,512]{2,1,0:T(8,128)S(1)} %get-tuple-element.7, f32[32,8,512]{2,1,0:T(8,128)S(1)} %copy-done, f32[32,8,512]{2,1,0:T(8,128)S(1)} %get-tuple-element.6, f32[]{:T(128)} %bitcast.1, f32[]{:T(128)} %bitcast), kind=kLoop, calls=%fused_computation | loop fusion | flops 917504 | bytes 2621448 | tf_op jit(solution)/shard_map/add | solution.py:413
Async XLA Ops:
  0.6 1.0 %copy-start = (f32[32,8,512]{2,1,0:T(8,128)S(1)}, f32[32,8,512]{2,1,0:T(8,128)}, u32[]{:S(2)}) copy-start(f32[32,8,512]{2,1,0:T(8,128)} %right_ref.1) | copy-start | bytes 1572868
  1.7 0.7 %copy-start.1 = (f32[8,512]{1,0:T(8,128)S(1)}, f32[8,512]{1,0:T(8,128)}, u32[]{:S(2)}) copy-start(f32[8,512]{1,0:T(8,128)} %kappa_ref.1) | copy-start | bytes 49156
  2.4 0.7 %copy-start.2 = (s32[8,512]{1,0:T(8,128)S(1)}, s32[8,512]{1,0:T(8,128)}, u32[]{:S(2)}) copy-start(s32[8,512]{1,0:T(8,128)} %mask_ref.1) | copy-start | bytes 49156
  3.1 0.7 %copy-start.3 = (f32[5,32]{1,0:T(8,128)S(1)}, f32[5,32]{1,0:T(8,128)}, u32[]{:S(2)}) copy-start(f32[5,32]{1,0:T(8,128)} %band_ref.1) | copy-start | bytes 1924
  3.8 0.7 %copy-start.4 = (f32[32]{0:T(128)S(1)}, f32[32]{0:T(128)}, u32[]{:S(2)}) copy-start(f32[32]{0:T(128)} %nugget_ref.1) | copy-start | bytes 388
  4.5 0.7 %copy-start.5 = (s32[8]{0:T(128)S(1)}, s32[8]{0:T(128)}, u32[]{:S(2)}) copy-start(s32[8]{0:T(128)} %taper_ref.1) | copy-start | bytes 100

commit v2 on v1

--- a/solution.py
+++ b/solution.py
@@ -10,7 +10,7 @@
 TAPER_HOURS = 8
 LAG = 4
 RIM = 2
-LOW = 4
+LOW = 16
 
 SPDE_SCALE = 0.0625
 MESH = pl.DeviceIdType.MESH
@@ -24,14 +24,17 @@
     ns,
     nt,
     right_ref,
-    kappa_ref,
-    mask_ref,
+    kappa_hbm,
+    mask_hbm,
     nugget_ref,
     band_ref,
     taper_ref,
     q_out,
     w_ref,
-    coef_ref,
+    scale_1_ref,
+    scale_2_ref,
+    kappa_ref,
+    mask_ref,
     b_pad,
     b_rim,
     q_pad,
@@ -62,6 +65,10 @@
 
     load_b = pltpu.make_async_copy(right_ref, b_pad.at[pl.ds(LAG, hours)], local_sem.at[0])
     load_b.start()
+    load_kappa = pltpu.make_async_copy(kappa_hbm, kappa_ref, local_sem.at[2])
+    load_kappa.start()
+    load_mask = pltpu.make_async_copy(mask_hbm, mask_ref, local_sem.at[3])
+    load_mask.start()
 
     def near_partner(k):
         me = (s % low) * nt + t
@@ -120,6 +127,8 @@
     lax.fori_loop(0, hours, fill_band, 0)
 
     load_b.wait()
+    load_kappa.wait()
+    load_mask.wait()
     pl.semaphore_wait(barrier, greeted)
 
     row_of = {1: pl.ds(rows - RIM, RIM), -1: pl.ds(0, RIM)}
@@ -255,51 +264,48 @@
             out = out + x[:, c : c + 128]
         return out
 
-    def start_sum(which, buffers, sends, recvs, me, size, partner):
+    def whole(x):
+        return jnp.sum(jnp.sum(x, axis=0, keepdims=True), axis=1, keepdims=True)
+
+    def shift_of(norm, product):
+        return jnp.where(norm > 0.0, jnp.clip(product / norm, 0.0, 64.0), 0.0)
+
+    def packed(values):
+        tile = jnp.zeros((8, 128), jnp.float32)
+        for row, value in enumerate(values):
+            tile = jnp.where(lag_row == row, value, tile)
+        return tile
+
+    def gather(tile, slots, sends, recvs, me, size, partner):
+        slots[me] = tile
         copies = []
         for k in range(1, size):
             copy = pltpu.make_async_remote_copy(
-                src_ref=buffers.at[which, me],
-                dst_ref=buffers.at[which, me],
-                send_sem=sends.at[which, k],
-                recv_sem=recvs.at[which, k],
+                src_ref=slots.at[me],
+                dst_ref=slots.at[me],
+                send_sem=sends.at[k],
+                recv_sem=recvs.at[k],
                 device_id=partner(k),
                 device_id_type=MESH,
             )
             copy.start()
             copies.append(copy)
-        return copies
-
-    near_me = (s % low) * nt + t
-    far_me = s // low
-
-    def start_near(which, first, second):
-        one = jnp.sum(first, axis=0, keepdims=True)
-        two = jnp.sum(second, axis=0, keepdims=True)
-        value = jnp.where(lag_row == 0, one, jnp.where(lag_row == 1, two, 0.0))
-        sum_near[which, near_me] = value
-        return start_sum(which, sum_near, near_send, near_recv, near_me, near, near_partner)
-
-    def finish_near(which, copies):
         for copy in copies:
             copy.wait()
-        total = sum_near[which, 0]
-        for k in range(1, near):
-            total = total + sum_near[which, k]
-        return total
-
-    def start_far(which, value):
-        sum_far[which, far_me] = value
-        return start_sum(which, sum_far, far_send, far_recv, far_me, far, far_partner)
-
-    def finish_far(which, copies):
-        for copy in copies:
-            copy.wait()
-        total = sum_far[which, 0]
-        for k in range(1, far):
-            total = total + sum_far[which, k]
-        total = jnp.sum(total, axis=1, keepdims=True)
-        return total[0:1, :], total[1:2, :]
+
+    def merged(slots, size, shift_from):
+        parts = [[slots[k, row : row + 1, :] for row in range(7)] for k in range(size)]
+        norm = sum(p[0] for p in parts)
+        product = sum(p[1] for p in parts)
+        shift = shift_from(norm, product)
+        square = cross = image_sum = mutual = 0.0
+        for bb, bq, ee, eb, ef, eq, own in parts:
+            d = own - shift
+            square = square + (ee + d * (2.0 * eb + d * bb))
+            cross = cross + (eb + d * bb)
+            image_sum = image_sum + (ef + d * (eq + d * bq))
+            mutual = mutual + (eq + 2.0 * d * bq)
+        return [norm, product, square, cross, image_sum, mutual, shift]
 
     wait_halo(0, b_pad, b_rim, True)
     for ds, dt, copy in aux_copies():
@@ -322,7 +328,6 @@
     norm, product = lax.fori_loop(0, hours, first_step, (zero, zero), unroll=2)
 
     start_halo(1, q_pad, q_rim)
-    copies = start_near(0, norm, product)
     store_q = pltpu.make_async_copy(q_pad.at[pl.ds(LAG, hours)], q_out, local_sem.at[1])
     store_q.start()
     drain_halo(0, b_pad, b_rim)
@@ -332,36 +337,50 @@
         def _():
             copy.wait_send()
 
+    norm = whole(norm)
+    product = whole(product)
+    shift = shift_of(norm, product)
     wait_halo(1, q_pad, q_rim, True)
-    value = finish_near(0, copies)
-    copies = start_far(0, value)
     mix_hours(q_pad)
-    norm_0, product_0 = finish_far(0, copies)
-    step_0 = norm_0 / product_0
     wait_halo(1, q_pad, q_rim, False)
 
     def second_step(h, carry):
-        norm, product = carry
+        square, cross, image_sum, mutual = carry
+        b = b_pad[LAG + h]
         q = q_pad[LAG + h]
         value = image(q_pad, q_rim, h)
         w_ref[h] = value
-        left = b_pad[LAG + h] - step_0 * q
-        left_image = q - step_0 * value
-        return norm + fold(left * left), product + fold(left * left_image)
-
-    norm, product = lax.fori_loop(0, hours, second_step, (zero, zero), unroll=2)
-    copies = start_near(1, norm, product)
+        left = q - shift * b
+        left_image = value - shift * q
+        return (
+            square + fold(left * left),
+            cross + fold(left * b),
+            image_sum + fold(left * left_image),
+            mutual + fold(left * q + b * left_image),
+        )
+
+    sums = lax.fori_loop(0, hours, second_step, (zero,) * 4, unroll=2)
+    tile = packed([norm, product] + [whole(x) for x in sums] + [shift])
+    if far > 1:
+        gather(tile, sum_near, near_send, near_recv, (s % low) * nt + t, near, near_partner)
+        tile = packed(merged(sum_near, near, shift_of))
+        gather(tile, sum_far, far_send, far_recv, s // low, far, far_partner)
+        total = merged(sum_far, far, lambda x, y: y / x)
+    else:
+        gather(tile, sum_near, near_send, near_recv, (s % low) * nt + t, near, near_partner)
+        total = merged(sum_near, near, lambda x, y: y / x)
     drain_halo(1, q_pad, q_rim)
     store_q.wait()
-    value = finish_near(1, copies)
-    copies = start_far(1, value)
-    norm_1, product_1 = finish_far(1, copies)
-
-    ratio = norm_1 / norm_0
-    step_1 = norm_1 / (product_1 - ratio * norm_1 / step_0)
+
+    norm, product, square, _, image_sum, _, _ = total
+    step_0 = norm / product
+    part = square / product
+    ratio = step_0 * part
+    step_1 = square / (image_sum - square * part)
     scale_1 = step_0 + step_1 * (1.0 + ratio)
     scale_2 = step_1 * step_0
-    coef_ref[...] = jnp.where(lag_row == 0, scale_1, scale_2)
+    for scale, ref in ((scale_1, scale_1_ref), (scale_2, scale_2_ref)):
+        ref[...] = jnp.broadcast_to(jnp.concatenate([scale] * (cols // 128), axis=1), (rows, cols))
 
 
 def body(ns, nt, right_side, kappa_field, land_mask, nugget, time_band, taper_width):
@@ -374,12 +393,15 @@
     smem = pl.BlockSpec(memory_space=pltpu.SMEM)
     hbm = pl.BlockSpec(memory_space=pl.ANY)
     field = jax.ShapeDtypeStruct(right_side.shape, jnp.float32)
-    q, w, coef = pl.pallas_call(
+    plane = jax.ShapeDtypeStruct((rows, cols), jnp.float32)
+    q, w, scale_1, scale_2 = pl.pallas_call(
         functools.partial(kernel, ns, nt),
-        out_shape=(field, field, jax.ShapeDtypeStruct((8, 128), jnp.float32)),
-        in_specs=[hbm, vmem, vmem, smem, smem, smem],
-        out_specs=(hbm, vmem, vmem),
+        out_shape=(field, field, plane, plane),
+        in_specs=[hbm, hbm, hbm, smem, smem, smem],
+        out_specs=(hbm, vmem, vmem, vmem),
         scratch_shapes=[
+            pltpu.VMEM((rows, cols), jnp.float32),
+            pltpu.VMEM((rows, cols), jnp.int32),
             padded,
             padded,
             padded,
@@ -387,27 +409,25 @@
             pltpu.VMEM((hours, rows, cols), jnp.float32),
             pltpu.VMEM((hours + LAG, 8, 128), jnp.float32),
             pltpu.VMEM((rows, cols), jnp.float32),
-            pltpu.VMEM((2, near, 8, 128), jnp.float32),
-            pltpu.VMEM((2, far, 8, 128), jnp.float32),
-            pltpu.SemaphoreType.DMA((2,)),
+            pltpu.VMEM((near, 8, 128), jnp.float32),
+            pltpu.VMEM((far, 8, 128), jnp.float32),
+            pltpu.SemaphoreType.DMA((4,)),
             pltpu.SemaphoreType.DMA((2, 8)),
             pltpu.SemaphoreType.DMA((2, 8)),
             pltpu.SemaphoreType.DMA((3,)),
             pltpu.SemaphoreType.DMA((3,)),
-            pltpu.SemaphoreType.DMA((2, near)),
-            pltpu.SemaphoreType.DMA((2, near)),
-            pltpu.SemaphoreType.DMA((2, far)),
-            pltpu.SemaphoreType.DMA((2, far)),
+            pltpu.SemaphoreType.DMA((near,)),
+            pltpu.SemaphoreType.DMA((near,)),
+            pltpu.SemaphoreType.DMA((far,)),
+            pltpu.SemaphoreType.DMA((far,)),
         ],
         compiler_params=pltpu.CompilerParams(
-            collective_id=0, has_side_effects=True, vmem_limit_bytes=32 * 1024 * 1024
+            collective_id=0, has_side_effects=True, vmem_limit_bytes=60 * 1024 * 1024
         ),
         cost_estimate=pl.CostEstimate(
             flops=200 * right_side.size, bytes_accessed=12 * right_side.size, transcendentals=0
         ),
     )(right_side, kappa_field, land_mask, nugget, time_band, taper_width)
-    scale_1 = coef[0, 0]
-    scale_2 = coef[1, 0]
     return (
         scale_1 * right_side - scale_2 * q,
         right_side - scale_1 * q + scale_2 * w,

time: 48.5 us -> 39.1 us (0.81)
  local copies, waits for them, and re-layouts: 5.05 us -> 0.01 us
  Pallas kernels: 40 us -> 36 us
    unnamed x12 -> x2, local copies, waits for them, and re-layouts: 4.46 us -> 0.01 us
    pallas_call x1, Pallas kernels: 40 us -> 36 us  [body(): pl.pallas_call(functools.partial(kernel, ns, nt), out_shape=(field, field...]
    slice x1 -> x0, local copies, waits for them, and re-layouts: 0.58 us -> none  [body(): scale_1 = coef[0, 0]]
where the time goes in v2:
time: 39.1 us; the launch traced here: 39 us
  Pallas kernels  36 us (92%)
  other arithmetic  2.35 us (6%)
  between operations  0.66 us (2%)
    pallas_call x1, Pallas kernels, body(): pl.pallas_call(functools.partial(kernel, ns, nt), out_shape=(field, field...  36 us
    add x1, other arithmetic, body(): right_side - scale_1 * q + scale_2 * w  2.35 us

profile of v2, /device:TPU:0, one launch (start us, length us, event | category | flops | bytes accessed | tf_op | source)
XLA Modules:
  0.0 39.0 jit_solution(16377943021964537850)
XLA Ops:
  0.6 0.0 copy-start
  0.6 36.0 %shard_map.77 = (f32[32,8,512]{2,1,0:T(8,128)}, f32[32,8,512]{2,1,0:T(8,128)}, f32[8,512]{1,0:T(8,128)}, f32[8,512]{1,0:T(8,128)}) custom-call(f32[32,8,512]{2,1,0:T(8,128)} %right_ref.1, f32[8,512]{1,0:T(8,128)} %kappa_hbm.1, s32[8,512]{1,0:T(8,128)} %mask_hbm.1, f32[32]{0:T(128)} %nugget_ref.1, f32[5,32]{1,0:T(8,128)} %band_ref.1, s32[8]{0:T(128)} %taper_ref.1), custom_call_target="tpu_custom_call" | custom-call | flops 26214400 | bytes 1572864 | tf_op jit(solution)/shard_map/pallas_call | solution.py:397
  36.6 0.0 copy-done
  36.6 2.4 %multiply_add_fusion = (f32[32,8,512]{2,1,0:T(8,128)}, f32[32,8,512]{2,1,0:T(8,128)}) fusion(f32[32,8,512]{2,1,0:T(8,128)} %get-tuple-element.9, f32[32,8,512]{2,1,0:T(8,128)S(1)} %copy-done, f32[32,8,512]{2,1,0:T(8,128)} %get-tuple-element.8, f32[8,512]{1,0:T(8,128)} %get-tuple-element.7, f32[8,512]{1,0:T(8,128)} %get-tuple-element.6), kind=kLoop, calls=%fused_computation | loop fusion | flops 917504 | bytes 2654208 | tf_op jit(solution)/shard_map/add | solution.py:433
Async XLA Ops:
  0.6 36.0 %copy-start = (f32[32,8,512]{2,1,0:T(8,128)S(1)}, f32[32,8,512]{2,1,0:T(8,128)}, u32[]{:S(2)}) copy-start(f32[32,8,512]{2,1,0:T(8,128)} %right_ref.1) | copy-start | bytes 1572868

commit v3 on v2

--- a/solution.py
+++ b/solution.py
@@ -11,13 +11,14 @@
 LAG = 4
 RIM = 2
 LOW = 16
+CHUNKS = 4
 
 SPDE_SCALE = 0.0625
 MESH = pl.DeviceIdType.MESH
 
 
 def halo_offsets():
-    return [(1, 0), (-1, 0), (1, 1), (1, -1), (-1, 1), (-1, -1), (0, 1), (0, -1)]
+    return [(0, 1), (0, -1), (1, 1), (1, -1), (-1, 1), (-1, -1), (1, 0), (-1, 0)]
 
 
 def kernel(
@@ -53,6 +54,8 @@
     near_recv,
     far_send,
     far_recv,
+    chunk_send,
+    chunk_recv,
 ):
     s = lax.axis_index("space")
     t = lax.axis_index("tm")
@@ -62,6 +65,7 @@
     low = min(LOW, ns)
     near = low * nt
     far = ns // low
+    size = hours // CHUNKS
 
     load_b = pltpu.make_async_copy(right_ref, b_pad.at[pl.ds(LAG, hours)], local_sem.at[0])
     load_b.start()
@@ -181,29 +185,67 @@
         ))
         return out
 
-    def start_halo(which, pad, rim):
+    def chunk_copy(which, side, chunk, pad, rim):
+        ds = (1, -1)[side]
+        span = pl.ds(LAG + chunk * size, size)
+        return pltpu.make_async_remote_copy(
+            src_ref=pad.at[span, row_of[ds]],
+            dst_ref=rim.at[span, row_of[ds]],
+            send_sem=chunk_send.at[which, side, chunk],
+            recv_sem=chunk_recv.at[which, side, chunk],
+            device_id=(s + ds, t),
+            device_id_type=MESH,
+        )
+
+    def start_edges(which, pad, rim, along):
         for index, (ds, dt) in enumerate(halo_offsets()):
-
-            @pl.when(exists(ds, dt))
-            def _():
-                halo_copy(which, index, pad, rim).start()
-
-    def wait_halo(which, pad, rim, along_hours):
+            if dt == along:
+
+                @pl.when(exists(ds, dt))
+                def _():
+                    halo_copy(which, index, pad, rim).start()
+
+    def wait_edges(which, pad, rim, along, strips):
         for index, (ds, dt) in enumerate(halo_offsets()):
-            if (ds == 0) == along_hours:
+            if dt == along and (ds != 0) == strips:
 
                 @pl.when(exists(-ds, -dt))
                 def _():
                     halo_copy(which, index, pad, rim).wait_recv()
 
+    def start_chunk(which, chunk, pad, rim):
+        for side, ds in enumerate((1, -1)):
+
+            @pl.when(exists(ds, 0))
+            def _():
+                chunk_copy(which, side, chunk, pad, rim).start()
+
+    def wait_chunk(which, chunk, pad, rim):
+        for side, ds in enumerate((1, -1)):
+
+            @pl.when(exists(-ds, 0))
+            def _():
+                chunk_copy(which, side, chunk, pad, rim).wait_recv()
+
     def drain_halo(which, pad, rim):
         for index, (ds, dt) in enumerate(halo_offsets()):
-
-            @pl.when(exists(ds, dt))
-            def _():
-                halo_copy(which, index, pad, rim).wait_send()
-
-    start_halo(0, b_pad, b_rim)
+            if dt:
+
+                @pl.when(exists(ds, dt))
+                def _():
+                    halo_copy(which, index, pad, rim).wait_send()
+
+        for chunk in range(CHUNKS):
+            for side, ds in enumerate((1, -1)):
+
+                @pl.when(exists(ds, 0))
+                def _():
+                    chunk_copy(which, side, chunk, pad, rim).wait_send()
+
+    start_edges(0, b_pad, b_rim, 1)
+    start_edges(0, b_pad, b_rim, -1)
+    for chunk in range(CHUNKS):
+        start_chunk(0, chunk, b_pad, b_rim)
     for ds, dt, copy in aux_copies():
 
         @pl.when(exists(ds, dt))
@@ -237,12 +279,12 @@
         right = jnp.where(last_col, 0.0, pltpu.roll(x, cols - 1, 1))
         return kappa4 * x - ((above + below) + (left + right))
 
-    def mix_hours(pad):
+    def mix_hours(pad, first, last):
         def step(h, carry):
             mixed[h] = along_time(pad, h)
             return carry
 
-        lax.fori_loop(0, hours, step, 0, unroll=2)
+        lax.fori_loop(first, last, step, 0, unroll=2)
 
     def image(pad, rim, h):
         x = mixed[h]
@@ -307,15 +349,15 @@
             mutual = mutual + (eq + 2.0 * d * bq)
         return [norm, product, square, cross, image_sum, mutual, shift]
 
-    wait_halo(0, b_pad, b_rim, True)
+    wait_edges(0, b_pad, b_rim, 1, False)
+    wait_edges(0, b_pad, b_rim, -1, False)
     for ds, dt, copy in aux_copies():
 
         @pl.when(exists(-ds, -dt))
         def _():
             copy.wait_recv()
 
-    mix_hours(b_pad)
-    wait_halo(0, b_pad, b_rim, False)
+    mix_hours(b_pad, 0, hours)
 
     def first_step(h, carry):
         norm, product = carry
@@ -325,9 +367,23 @@
         return norm + fold(b * b), product + fold(b * value)
 
     zero = jnp.zeros((rows, 128), jnp.float32)
-    norm, product = lax.fori_loop(0, hours, first_step, (zero, zero), unroll=2)
-
-    start_halo(1, q_pad, q_rim)
+    norm, product = zero, zero
+    wait_edges(0, b_pad, b_rim, 1, True)
+    wait_chunk(0, 0, b_pad, b_rim)
+    for chunk in range(CHUNKS):
+        if chunk + 1 < CHUNKS:
+            wait_chunk(0, chunk + 1, b_pad, b_rim)
+        else:
+            wait_edges(0, b_pad, b_rim, -1, True)
+        norm, product = lax.fori_loop(
+            chunk * size, (chunk + 1) * size, first_step, (norm, product), unroll=2
+        )
+        if chunk == 0:
+            start_edges(1, q_pad, q_rim, -1)
+        if chunk == CHUNKS - 1:
+            start_edges(1, q_pad, q_rim, 1)
+        start_chunk(1, chunk, q_pad, q_rim)
+
     store_q = pltpu.make_async_copy(q_pad.at[pl.ds(LAG, hours)], q_out, local_sem.at[1])
     store_q.start()
     drain_halo(0, b_pad, b_rim)
@@ -340,9 +396,11 @@
     norm = whole(norm)
     product = whole(product)
     shift = shift_of(norm, product)
-    wait_halo(1, q_pad, q_rim, True)
-    mix_hours(q_pad)
-    wait_halo(1, q_pad, q_rim, False)
+    mix_hours(q_pad, size, hours - size)
+    wait_edges(1, q_pad, q_rim, -1, False)
+    mix_hours(q_pad, hours - size, hours)
+    wait_edges(1, q_pad, q_rim, 1, False)
+    mix_hours(q_pad, 0, size)
 
     def second_step(h, carry):
         square, cross, image_sum, mutual = carry
@@ -359,7 +417,17 @@
             mutual + fold(left * q + b * left_image),
         )
 
-    sums = lax.fori_loop(0, hours, second_step, (zero,) * 4, unroll=2)
+    sums = (zero,) * 4
+    wait_chunk(1, 0, q_pad, q_rim)
+    wait_chunk(1, 1, q_pad, q_rim)
+    for chunk in list(range(1, CHUNKS)) + [0]:
+        if chunk == 0:
+            wait_edges(1, q_pad, q_rim, 1, True)
+        elif chunk + 1 < CHUNKS:
+            wait_chunk(1, chunk + 1, q_pad, q_rim)
+        else:
+            wait_edges(1, q_pad, q_rim, -1, True)
+        sums = lax.fori_loop(chunk * size, (chunk + 1) * size, second_step, sums, unroll=2)
     tile = packed([norm, product] + [whole(x) for x in sums] + [shift])
     if far > 1:
         gather(tile, sum_near, near_send, near_recv, (s % low) * nt + t, near, near_partner)
@@ -420,6 +488,8 @@
             pltpu.SemaphoreType.DMA((near,)),
             pltpu.SemaphoreType.DMA((far,)),
             pltpu.SemaphoreType.DMA((far,)),
+            pltpu.SemaphoreType.DMA((2, 2, CHUNKS)),
+            pltpu.SemaphoreType.DMA((2, 2, CHUNKS)),
         ],
         compiler_params=pltpu.CompilerParams(
             collective_id=0, has_side_effects=True, vmem_limit_bytes=60 * 1024 * 1024

time: 39.1 us -> 36.7 us (0.939)
  Pallas kernels: 36 us -> 33.5 us
    pallas_call x1, Pallas kernels: 36 us -> 33.5 us  [body(): pl.pallas_call(functools.partial(kernel, ns, nt), out_shape=(field, field...]
where the time goes in v3:
time: 36.7 us; the launch traced here: 36.6 us
  Pallas kernels  33.5 us (91%)
  other arithmetic  2.35 us (6%)
  between operations  0.66 us (2%)
    pallas_call x1, Pallas kernels, body(): pl.pallas_call(functools.partial(kernel, ns, nt), out_shape=(field, field...  33.5 us
    add x1, other arithmetic, body(): right_side - scale_1 * q + scale_2 * w  2.35 us

profile of v3, /device:TPU:0, one launch (start us, length us, event | category | flops | bytes accessed | tf_op | source)
XLA Modules:
  0.0 36.6 jit_solution(15264459813680590006)
XLA Ops:
  0.6 0.0 copy-start
  0.6 33.5 %shard_map.77 = (f32[32,8,512]{2,1,0:T(8,128)}, f32[32,8,512]{2,1,0:T(8,128)}, f32[8,512]{1,0:T(8,128)}, f32[8,512]{1,0:T(8,128)}) custom-call(f32[32,8,512]{2,1,0:T(8,128)} %right_ref.1, f32[8,512]{1,0:T(8,128)} %kappa_hbm.1, s32[8,512]{1,0:T(8,128)} %mask_hbm.1, f32[32]{0:T(128)} %nugget_ref.1, f32[5,32]{1,0:T(8,128)} %band_ref.1, s32[8]{0:T(128)} %taper_ref.1), custom_call_target="tpu_custom_call" | custom-call | flops 26214400 | bytes 1572864 | tf_op jit(solution)/shard_map/pallas_call | solution.py:465
  34.2 0.0 copy-done
  34.2 2.4 %multiply_add_fusion = (f32[32,8,512]{2,1,0:T(8,128)}, f32[32,8,512]{2,1,0:T(8,128)}) fusion(f32[32,8,512]{2,1,0:T(8,128)} %get-tuple-element.9, f32[32,8,512]{2,1,0:T(8,128)S(1)} %copy-done, f32[32,8,512]{2,1,0:T(8,128)} %get-tuple-element.8, f32[8,512]{1,0:T(8,128)} %get-tuple-element.7, f32[8,512]{1,0:T(8,128)} %get-tuple-element.6), kind=kLoop, calls=%fused_computation | loop fusion | flops 917504 | bytes 2654208 | tf_op jit(solution)/shard_map/add | solution.py:503
Async XLA Ops:
  0.6 33.6 %copy-start = (f32[32,8,512]{2,1,0:T(8,128)S(1)}, f32[32,8,512]{2,1,0:T(8,128)}, u32[]{:S(2)}) copy-start(f32[32,8,512]{2,1,0:T(8,128)} %right_ref.1) | copy-start | bytes 1572868

commit v4 on v3

--- a/solution.py
+++ b/solution.py
@@ -376,7 +376,7 @@
         else:
             wait_edges(0, b_pad, b_rim, -1, True)
         norm, product = lax.fori_loop(
-            chunk * size, (chunk + 1) * size, first_step, (norm, product), unroll=2
+            chunk * size, (chunk + 1) * size, first_step, (norm, product), unroll=4
         )
         if chunk == 0:
             start_edges(1, q_pad, q_rim, -1)
@@ -427,7 +427,7 @@
             wait_chunk(1, chunk + 1, q_pad, q_rim)
         else:
             wait_edges(1, q_pad, q_rim, -1, True)
-        sums = lax.fori_loop(chunk * size, (chunk + 1) * size, second_step, sums, unroll=2)
+        sums = lax.fori_loop(chunk * size, (chunk + 1) * size, second_step, sums, unroll=4)
     tile = packed([norm, product] + [whole(x) for x in sums] + [shift])
     if far > 1:
         gather(tile, sum_near, near_send, near_recv, (s % low) * nt + t, near, near_partner)

time: 36.7 us -> 35.5 us (0.967)
  Pallas kernels: 33.5 us -> 32.3 us
    pallas_call x1, Pallas kernels: 33.5 us -> 32.3 us  [body(): pl.pallas_call(functools.partial(kernel, ns, nt), out_shape=(field, field...]
where the time goes in v4:
time: 35.5 us; the launch traced here: 35.3 us
  Pallas kernels  32.3 us (91%)
  other arithmetic  2.35 us (7%)
  between operations  0.66 us (2%)
    pallas_call x1, Pallas kernels, body(): pl.pallas_call(functools.partial(kernel, ns, nt), out_shape=(field, field...  32.3 us
    add x1, other arithmetic, body(): right_side - scale_1 * q + scale_2 * w  2.35 us

profile of v4, /device:TPU:0, one launch (start us, length us, event | category | flops | bytes accessed | tf_op | source)
XLA Modules:
  0.0 35.3 jit_solution(9482247116780361949)
XLA Ops:
  0.6 0.0 copy-start
  0.6 32.3 %shard_map.77 = (f32[32,8,512]{2,1,0:T(8,128)}, f32[32,8,512]{2,1,0:T(8,128)}, f32[8,512]{1,0:T(8,128)}, f32[8,512]{1,0:T(8,128)}) custom-call(f32[32,8,512]{2,1,0:T(8,128)} %right_ref.1, f32[8,512]{1,0:T(8,128)} %kappa_hbm.1, s32[8,512]{1,0:T(8,128)} %mask_hbm.1, f32[32]{0:T(128)} %nugget_ref.1, f32[5,32]{1,0:T(8,128)} %band_ref.1, s32[8]{0:T(128)} %taper_ref.1), custom_call_target="tpu_custom_call" | custom-call | flops 26214400 | bytes 1572864 | tf_op jit(solution)/shard_map/pallas_call | solution.py:465
  33.0 0.0 copy-done
  33.0 2.4 %multiply_add_fusion = (f32[32,8,512]{2,1,0:T(8,128)}, f32[32,8,512]{2,1,0:T(8,128)}) fusion(f32[32,8,512]{2,1,0:T(8,128)} %get-tuple-element.9, f32[32,8,512]{2,1,0:T(8,128)S(1)} %copy-done, f32[32,8,512]{2,1,0:T(8,128)} %get-tuple-element.8, f32[8,512]{1,0:T(8,128)} %get-tuple-element.7, f32[8,512]{1,0:T(8,128)} %get-tuple-element.6), kind=kLoop, calls=%fused_computation | loop fusion | flops 917504 | bytes 2654208 | tf_op jit(solution)/shard_map/add | solution.py:503
Async XLA Ops:
  0.6 32.3 %copy-start = (f32[32,8,512]{2,1,0:T(8,128)S(1)}, f32[32,8,512]{2,1,0:T(8,128)}, u32[]{:S(2)}) copy-start(f32[32,8,512]{2,1,0:T(8,128)} %right_ref.1) | copy-start | bytes 1572868
